TPU v7x, 32 devices: a whole 2x2x4 slice. The times are simulated.
32 devices in a mesh: rep: 8 (over z, y), shard: 4 (over x, core).
Axes of the slice: x: 2, y: 2, z: 4, core: 2. Of those that a mesh axis runs over, the one named last changes fastest.
Arguments:
- inputs: bfloat16 [64, 1024, 512], P(('rep', 'shard')), may hold values from -6 to 6
- lengths: int32 [64], P(('rep', 'shard')), may hold values from 256 to 1024, as said below
- w_qkv: bfloat16 [512, 1536], P('shard'), may hold values from -0.25 to 0.25
- w_out: bfloat16 [512, 512], P('shard'), may hold values from -2 to 2
- w_in: bfloat16 [512, 2048], P('shard'), may hold values from -0.25 to 0.25
- w_back: bfloat16 [2048, 512], P('shard'), may hold values from -0.125 to 0.125
- vectors: bfloat16 [32, 512], P('shard'), may hold values from -5 to 5
- cotangent: bfloat16 [64, 1024, 512], P(('rep', 'shard')), may hold values from -6 to 6
Outputs:
- output: bfloat16 [64, 1024, 512], P(('rep', 'shard'))
- grad_inputs: bfloat16 [64, 1024, 512], P(('rep', 'shard'))
- grad_qkv: float32 [512, 1536], P('shard')
- grad_out: float32 [512, 512], P('shard')
- grad_in: float32 [512, 2048], P('shard')
- grad_back: float32 [2048, 512], P('shard')
- grad_vectors: float32 [32, 512], P('shard')
Inputs may be any that keep to these rules, and one draw needn't show every extreme that they name: `lengths`: valid tokens are a sequence's first slots; some sequence has exactly 1024 and some exactly 256.
All inputs are finite; a program needn't handle non-finite values.
Results may differ from a plain program's by a relative error of at most 0.019.
Values may be sent and summed in bfloat16 or wider, within the bound.
No kernel may reach another device: no remote copies, remote signals or barrier semaphores. Data moves between devices by JAX's collectives and lax.ppermute only.
A program may use at most 192 MiB of HBM per device.

v0:
```python
from functools import partial

import jax
import jax.numpy as jnp
from jax import lax
from jax.sharding import PartitionSpec as P

D = 512
HEADS = 8
HDIM = 64
FF = 2048
MEM = 20


def unpack_rows(rows):
    floats = rows.astype(jnp.float32)
    blocks = FF // D
    return (
        rows[:MEM],
        floats[MEM],
        floats[MEM + 1],
        floats[MEM + 2],
        floats[MEM + 3 : MEM + 3 + blocks].reshape(FF),
        floats[MEM + 3 + blocks],
        floats[MEM + 4 + blocks],
        floats[MEM + 5 + blocks],
        floats[MEM + 6 + blocks],
        floats[MEM + 7 + blocks],
    )


def norm_forward(values):
    center = values - jnp.mean(values, axis=-1, keepdims=True)
    inverse = lax.rsqrt(jnp.mean(center * center, axis=-1, keepdims=True) + 1e-05)
    return (center * inverse, inverse)


def norm_backward(grad_normed, normed, inverse):
    return inverse * (
        grad_normed
        - jnp.mean(grad_normed, axis=-1, keepdims=True)
        - normed * jnp.mean(grad_normed * normed, axis=-1, keepdims=True)
    )


def gelu_tanh(values):
    return jax.nn.gelu(values, approximate=True)


def to_heads(matrix):
    return matrix.reshape(matrix.shape[0], HEADS, HDIM).transpose(1, 0, 2)


def from_heads(stack):
    return stack.transpose(1, 0, 2).reshape(stack.shape[1], D)


def head_scores(query_head, key_head, key_mask):
    raw = jnp.einsum(
        "qd,kd->qk", query_head, key_head, preferred_element_type=jnp.float32
    ) * HDIM ** (-0.5)
    return jnp.where(key_mask[None, :], raw, -1e30)


def forward_one(weights, item):
    weight_qkv, weight_out, weight_in, weight_back, rows = weights
    tokens, length = item
    (
        memory,
        bias_query,
        bias_value,
        bias_out,
        bias_in,
        bias_back,
        gain_one,
        shift_one,
        gain_two,
        shift_two,
    ) = unpack_rows(rows)
    seq_rows = tokens.shape[0]
    joined = jnp.concatenate([memory, tokens], 0)
    qkv_bias = jnp.concatenate([bias_query, jnp.zeros_like(bias_query), bias_value])
    projected = (jnp.dot(joined, weight_qkv, preferred_element_type=jnp.float32) + qkv_bias).astype(
        jnp.bfloat16
    )
    key_mask = jnp.arange(MEM + seq_rows, dtype=jnp.int32) < MEM + length

    def attend(head_items):
        query_head, key_head, value_head = head_items
        scores = head_scores(query_head, key_head, key_mask)
        top = jnp.max(scores, axis=-1, keepdims=True)
        expo = jnp.exp(scores - top)
        total = jnp.sum(expo, axis=-1, keepdims=True)
        soft_rows = (expo / total).astype(jnp.bfloat16)
        head_mixed = jnp.dot(soft_rows, value_head, preferred_element_type=jnp.float32)
        return (head_mixed, (top + jnp.log(total))[:, 0])

    head_out, log_total = lax.map(
        attend,
        (
            to_heads(projected[MEM:, :D]),
            to_heads(projected[:, D : 2 * D]),
            to_heads(projected[:, 2 * D :]),
        ),
    )
    mixed = from_heads(head_out).astype(jnp.bfloat16)
    attn = jnp.dot(mixed, weight_out, preferred_element_type=jnp.float32) + bias_out
    normed_one, inverse_one = norm_forward(tokens.astype(jnp.float32) + attn)
    first = normed_one * gain_one + shift_one
    up_value = (
        jnp.dot(first.astype(jnp.bfloat16), weight_in, preferred_element_type=jnp.float32) + bias_in
    )
    activated, pull_gelu = jax.vjp(gelu_tanh, up_value)
    slope = pull_gelu(jnp.ones_like(up_value))[0]
    active = activated.astype(jnp.bfloat16)
    down_value = jnp.dot(active, weight_back, preferred_element_type=jnp.float32) + bias_back
    normed_two, inverse_two = norm_forward(first + down_value)
    valid = (jnp.arange(seq_rows, dtype=jnp.int32) < length).astype(jnp.float32)[:, None]
    result = ((normed_two * gain_two + shift_two) * valid).astype(jnp.bfloat16)
    return (
        result,
        (
            projected,
            log_total,
            mixed,
            normed_one,
            inverse_one,
            active,
            slope,
            normed_two,
            inverse_two,
        ),
    )


def backward_one(weights, carry, item):
    weight_qkv, weight_out, weight_in, weight_back, rows = weights
    (
        tokens,
        length,
        cot_rows,
        projected,
        log_total,
        mixed,
        normed_one,
        inverse_one,
        active,
        slope,
        normed_two,
        inverse_two,
    ) = item
    (
        memory,
        bias_query,
        bias_value,
        bias_out,
        bias_in,
        bias_back,
        gain_one,
        shift_one,
        gain_two,
        shift_two,
    ) = unpack_rows(rows)
    seq_rows = tokens.shape[0]
    valid = (jnp.arange(seq_rows, dtype=jnp.int32) < length).astype(jnp.float32)[:, None]
    grad_result = cot_rows.astype(jnp.float32) * valid
    term_gain_two = jnp.sum(grad_result * normed_two, axis=0)
    term_shift_two = jnp.sum(grad_result, axis=0)
    grad_second = norm_backward(grad_result * gain_two, normed_two, inverse_two)
    grad_down = grad_second.astype(jnp.bfloat16)
    term_bias_back = jnp.sum(grad_down.astype(jnp.float32), axis=0)
    term_back = jnp.einsum("lf,ld->fd", active, grad_down, preferred_element_type=jnp.float32)
    grad_active = jnp.einsum(
        "ld,fd->lf", grad_down, weight_back, preferred_element_type=jnp.float32
    )
    grad_up = (grad_active * slope).astype(jnp.bfloat16)
    term_bias_in = jnp.sum(grad_up.astype(jnp.float32), axis=0)
    first = normed_one * gain_one + shift_one
    term_in = jnp.einsum(
        "ld,lf->df", first.astype(jnp.bfloat16), grad_up, preferred_element_type=jnp.float32
    )
    grad_first = (
        jnp.einsum("lf,df->ld", grad_up, weight_in, preferred_element_type=jnp.float32)
        + grad_second
    )
    term_gain_one = jnp.sum(grad_first * normed_one, axis=0)
    term_shift_one = jnp.sum(grad_first, axis=0)
    grad_hone = norm_backward(grad_first * gain_one, normed_one, inverse_one)
    grad_attn = grad_hone.astype(jnp.bfloat16)
    term_bias_out = jnp.sum(grad_attn.astype(jnp.float32), axis=0)
    term_out = jnp.einsum("le,ld->ed", mixed, grad_attn, preferred_element_type=jnp.float32)
    grad_mixed = jnp.einsum(
        "ld,ed->le", grad_attn, weight_out, preferred_element_type=jnp.float32
    ).astype(jnp.bfloat16)
    key_mask = jnp.arange(MEM + seq_rows, dtype=jnp.int32) < MEM + length

    def attend_back(head_items):
        query_head, key_head, value_head, head_total, grad_head = head_items
        scores = head_scores(query_head, key_head, key_mask)
        probs = jnp.exp(scores - head_total[:, None])
        grad_probs = jnp.einsum(
            "qd,kd->qk", grad_head, value_head, preferred_element_type=jnp.float32
        )
        inner = jnp.sum(grad_probs * probs, axis=-1, keepdims=True)
        grad_scores = (probs * (grad_probs - inner)).astype(jnp.bfloat16)
        scale = HDIM ** (-0.5)
        grad_query = (
            jnp.einsum("qk,kd->qd", grad_scores, key_head, preferred_element_type=jnp.float32)
            * scale
        )
        grad_key = (
            jnp.einsum("qk,qd->kd", grad_scores, query_head, preferred_element_type=jnp.float32)
            * scale
        )
        grad_value = jnp.einsum(
            "qk,qd->kd", probs.astype(jnp.bfloat16), grad_head, preferred_element_type=jnp.float32
        )
        return (grad_query, grad_key, grad_value)

    grad_queries, grad_keys, grad_values = lax.map(
        attend_back,
        (
            to_heads(projected[MEM:, :D]),
            to_heads(projected[:, D : 2 * D]),
            to_heads(projected[:, 2 * D :]),
            log_total,
            to_heads(grad_mixed),
        ),
    )
    query_rows = jnp.concatenate([jnp.zeros((MEM, D), jnp.float32), from_heads(grad_queries)], 0)
    grad_proj = jnp.concatenate(
        [query_rows, from_heads(grad_keys), from_heads(grad_values)], 1
    ).astype(jnp.bfloat16)
    proj_sums = jnp.sum(grad_proj.astype(jnp.float32), axis=0)
    joined = jnp.concatenate([memory, tokens], 0)
    term_qkv = jnp.einsum("kd,ke->de", joined, grad_proj, preferred_element_type=jnp.float32)
    grad_joined = jnp.einsum("ke,de->kd", grad_proj, weight_qkv, preferred_element_type=jnp.float32)
    grad_tokens = (grad_joined[MEM:] + grad_hone).astype(jnp.bfloat16)
    terms = (
        term_qkv,
        term_out,
        term_in,
        term_back,
        grad_joined[:MEM],
        proj_sums[:D],
        proj_sums[2 * D :],
        term_bias_out,
        term_bias_in,
        term_bias_back,
        term_gain_one,
        term_shift_one,
        term_gain_two,
        term_shift_two,
    )
    updated = tuple((older + newer for older, newer in zip(carry, terms)))
    return (updated, grad_tokens)


def body(inputs, lengths, w_qkv, w_out, w_in, w_back, vectors, cotangent):
    gathered = (
        lax.all_gather(w_qkv, "shard", axis=0, tiled=True),
        lax.all_gather(w_out, "shard", axis=0, tiled=True),
        lax.all_gather(w_in, "shard", axis=0, tiled=True),
        lax.all_gather(w_back, "shard", axis=0, tiled=True),
        lax.all_gather(vectors, "shard", axis=0, tiled=True),
    )
    outputs, saved = lax.map(partial(forward_one, gathered), (inputs, lengths))
    weights_back = (
        lax.all_gather(w_qkv, "shard", axis=0, tiled=True),
        lax.all_gather(w_out, "shard", axis=0, tiled=True),
        lax.all_gather(w_in, "shard", axis=0, tiled=True),
        lax.all_gather(w_back, "shard", axis=0, tiled=True),
        lax.all_gather(vectors, "shard", axis=0, tiled=True),
    )
    zero_row = jnp.zeros((D,), jnp.float32)
    initial = (
        jnp.zeros((D, 3 * D), jnp.float32),
        jnp.zeros((D, D), jnp.float32),
        jnp.zeros((D, FF), jnp.float32),
        jnp.zeros((FF, D), jnp.float32),
        jnp.zeros((MEM, D), jnp.float32),
        zero_row,
        zero_row,
        zero_row,
        jnp.zeros((FF,), jnp.float32),
        zero_row,
        zero_row,
        zero_row,
        zero_row,
        zero_row,
    )
    totals, grad_inputs = lax.scan(
        partial(backward_one, weights_back), initial, (inputs, lengths, cotangent) + saved
    )
    grad_rows = jnp.concatenate(
        [
            totals[4],
            totals[5][None],
            totals[6][None],
            totals[7][None],
            totals[8].reshape(FF // D, D),
            totals[9][None],
            totals[10][None],
            totals[11][None],
            totals[12][None],
            totals[13][None],
        ],
        0,
    )
    pieces = (
        lax.psum_scatter(
            totals[0].astype(jnp.bfloat16), "shard", scatter_dimension=0, tiled=True
        ).astype(jnp.float32),
        lax.psum_scatter(
            totals[1].astype(jnp.bfloat16), "shard", scatter_dimension=0, tiled=True
        ).astype(jnp.float32),
        lax.psum_scatter(
            totals[2].astype(jnp.bfloat16), "shard", scatter_dimension=0, tiled=True
        ).astype(jnp.float32),
        lax.psum_scatter(
            totals[3].astype(jnp.bfloat16), "shard", scatter_dimension=0, tiled=True
        ).astype(jnp.float32),
        lax.psum_scatter(
            grad_rows.astype(jnp.bfloat16), "shard", scatter_dimension=0, tiled=True
        ).astype(jnp.float32),
    )
    summed = (
        lax.psum(pieces[0].astype(jnp.bfloat16), "rep").astype(jnp.float32),
        lax.psum(pieces[1].astype(jnp.bfloat16), "rep").astype(jnp.float32),
        lax.psum(pieces[2].astype(jnp.bfloat16), "rep").astype(jnp.float32),
        lax.psum(pieces[3].astype(jnp.bfloat16), "rep").astype(jnp.float32),
        lax.psum(pieces[4].astype(jnp.bfloat16), "rep").astype(jnp.float32),
    )
    return (outputs, grad_inputs, summed[0], summed[1], summed[2], summed[3], summed[4])


def solution(mesh):
    placed = (
        P(("rep", "shard"), None, None),
        P(("rep", "shard")),
        P("shard", None),
        P("shard", None),
        P("shard", None),
        P("shard", None),
        P("shard", None),
        P(("rep", "shard"), None, None),
    )
    return jax.shard_map(
        body,
        mesh=mesh,
        in_specs=placed,
        out_specs=(
            P(("rep", "shard"), None, None),
            P(("rep", "shard"), None, None),
            P("shard", None),
            P("shard", None),
            P("shard", None),
            P("shard", None),
            P("shard", None),
        ),
        check_vma=False,
    )
```

profile of v0, /device:TPU:0, one launch (start us, length us, event | category | flops | bytes accessed | tf_op | source)
XLA Modules:
  0.0 904.3 jit_solution(3299980023438510980)
XLA Ops:
  16.2 12.5 %all_gather.22 = bf16[512,512]{1,0:T(8,128)(2,1)} all-gather(bf16[128,512]{1,0:T(8,128)(2,1)} %param.19), channel_id=1, replica_groups=mesh['rep'=8,'shard'=4] {'shard'}, dimensions={0}, use_global_device_ids=true | all-gather | bytes 655360 | tf_op jit(solution)/shard_map/all_gather | solution.py:262
  34.5 24.5 %all-gather.6.cloned.1.call-done = bf16[512,2048]{1,0:T(8,128)(2,1)} async-done(((bf16[128,2048]{1,0:T(8,128)(2,1)}), bf16[512,2048]{1,0:T(8,128)(2,1)}) %all-gather.6.cloned.1.call-update) | async-done | bytes 2097168 | tf_op jit(solution)/shard_map/all_gather | solution.py:263
  58.9 24.2 %all-gather.8.cloned.1.call-done = bf16[2048,512]{1,0:T(8,128)(2,1)} async-done(((bf16[512,512]{1,0:T(8,128)(2,1)}), bf16[2048,512]{1,0:T(8,128)(2,1)}) %all-gather.8.cloned.1.call-update) | async-done | bytes 2097168 | tf_op jit(solution)/shard_map/all_gather | solution.py:264
  84.6 194.0 %while.111 = (s32[]{:T(128)}, bf16[2,1024,512]{2,1,0:T(8,128)(2,1)}, bf16[2,1044,1536]{2,1,0:T(8,128)(2,1)}, f32[2,8,1024]{2,1,0:T(8,128)}, bf16[2,1024,512]{1,2...) while((s32[]{:T(128)}, bf16[2,1024,512]{2,1,0:T(8,128)(2,1)}, ...), condition=%wide.region_9.10_spmd, body=%wide.region_0.9_spmd.sunk | while | flops 6857976832 | bytes 233697840 | solution.py:267
  101.6 48.3 %while.114 = (s32[]{:T(128)}, bf16[8,1024,64]{1,2,0:T(8,128)(2,1)S(1)}, f32[8,1024]{1,0:T(8,128)S(1)}, bf16[8,1024,64]{1,2,0:T(8,128)(2,1)S(1)}, bf16[8,1044,64]...) while((s32[]{:T(128)}, ...), condition=%wide.region_4.4_spmd.clone, body=%wide.region_1.3_spmd.clone.sunk | while | flops 282230784 | bytes 30684308 | solution.py:98
  154.1 8.3 bitcast_dynamic-update-slice_fusion.12
  162.4 6.8 fusion.208
  198.6 48.3 %while.114 = (s32[]{:T(128)}, bf16[8,1024,64]{1,2,0:T(8,128)(2,1)S(1)}, f32[8,1024]{1,0:T(8,128)S(1)}, bf16[8,1024,64]{1,2,0:T(8,128)(2,1)S(1)}, bf16[8,1044,64]...) while((s32[]{:T(128)}, ...), condition=%wide.region_4.4_spmd.clone, body=%wide.region_1.3_spmd.clone.sunk | while | flops 282230784 | bytes 30684308 | solution.py:98
  251.0 8.4 bitcast_dynamic-update-slice_fusion.12
  259.4 6.8 fusion.208
  280.0 371.7 %while.113 = (s32[]{:T(128)}, f32[512,1536]{1,0:T(8,128)}, f32[512,512]{1,0:T(8,128)}, f32[512,2048]{1,0:T(8,128)}, f32[2048,512]{1,0:T(8,128)}, /*index=5*/f32[...) while((s32[]{:T(128)}, f32[512,1536]{1,0:T(8,128)}, ...), condition=%wide.region_26.27_spmd.clone, body=%wide.region_10.26_spmd.clone.sunk | while | flops 13725964288 | bytes 392530816 | solution.py:292
  313.7 7.9 convert_reduce_fusion.9
  323.6 7.0 fusion.228
  351.1 87.4 %while.115 = (s32[]{:T(128)}, bf16[8,1024,64]{1,2,0:T(8,128)(2,1)}, bf16[8,1044,64]{1,2,0:T(8,128)(2,1)}, bf16[8,1044,64]{1,2,0:T(8,128)(2,1)}, bf16[8,1024,64]{...) while((s32[]{:T(128)}, bf16[8,1024,64]{1,2,0:T(8,128)(2,1)}, ...), condition=%wide.region_17.17_spmd.clone, body=%wide.region_15.16_spmd.clone.sunk | while | flops 693949696 | bytes 34189448 | solution.py:220
  488.6 7.9 convert_reduce_fusion.9
  498.4 7.0 fusion.228
  526.0 87.4 %while.115 = (s32[]{:T(128)}, bf16[8,1024,64]{1,2,0:T(8,128)(2,1)}, bf16[8,1044,64]{1,2,0:T(8,128)(2,1)}, bf16[8,1044,64]{1,2,0:T(8,128)(2,1)}, bf16[8,1024,64]{...) while((s32[]{:T(128)}, bf16[8,1024,64]{1,2,0:T(8,128)(2,1)}, ...), condition=%wide.region_17.17_spmd.clone, body=%wide.region_15.16_spmd.clone.sunk | while | flops 693949696 | bytes 34189448 | solution.py:220
  629.4 6.7 convolution_add_fusion.6
  675.6 30.7 %reduce-scatter.6.cloned.1.call-done = bf16[128,1536]{1,0:T(8,128)(2,1)} async-done(((bf16[512,1536]{1,0:T(8,128)(2,1)}), bf16[128,1536]{1,0:T(8,128)(2,1)}) %reduce-scatter.6.cloned.1.call-update) | async-done | bytes 393232 | tf_op jit(solution)/shard_map/reduce_scatter | solution.py:311
  706.4 33.9 %reduce-scatter.10.cloned.1.call-done = bf16[128,2048]{1,0:T(8,128)(2,1)} async-done(((bf16[512,2048]{1,0:T(8,128)(2,1)}), bf16[128,2048]{1,0:T(8,128)(2,1)}) %reduce-scatter.10.cloned.1.call-update) | async-done | bytes 524304 | tf_op jit(solution)/shard_map/reduce_scatter | solution.py:317
  740.3 34.2 %reduce-scatter.12.cloned.1.call-done = bf16[512,512]{1,0:T(8,128)(2,1)} async-done(((bf16[2048,512]{1,0:T(8,128)(2,1)}), bf16[512,512]{1,0:T(8,128)(2,1)}) %reduce-scatter.12.cloned.1.call-update) | async-done | bytes 524304 | tf_op jit(solution)/shard_map/reduce_scatter | solution.py:320
  774.4 22.3 %reduce-scatter.14.cloned.1.call-done = bf16[8,512]{1,0:T(8,128)(2,1)} async-done(((bf16[32,512]{1,0:T(8,128)(2,1)}), bf16[8,512]{1,0:T(8,128)(2,1)}) %reduce-scatter.14.cloned.1.call-update) | async-done | bytes 8208 | tf_op jit(solution)/shard_map/reduce_scatter | solution.py:323
  796.8 22.4 %psum.39 = bf16[8,512]{1,0:T(8,128)(2,1)S(1)} all-reduce(bf16[8,512]{1,0:T(8,128)(2,1)} %reduce-scatter.14.cloned.1.call-done), channel_id=1, replica_groups=mesh['rep'=8,'shard'=4] {'rep'}, use_global_device_ids=true, to_apply=%region_36.37 | all-reduce | flops 4096 | bytes 16384 | tf_op jit(solution)/shard_map/psum | solution.py:332
  819.8 71.6 %all-reduce.4.cloned.1.call-done = (bf16[128,1536]{1,0:T(8,128)(2,1)}, bf16[128,512]{1,0:T(8,128)(2,1)}, bf16[128,2048]{1,0:T(8,128)(2,1)}, bf16[512,512]{1,0:T(8,128)(2,1)}) async-done(((bf16[128,1536]{1,0:T(8,128)(2,1)}, bf16[128,512]{1,0:T(8,128)(2,1)}, bf16[128,2048]{1,0:T(8,128)(2,1)}, bf16[512,512]{1,0:T(8,128)(2,1)}), (bf16[128,1536]{1,0:T(8,128)(2,1)}, bf16[128,512]{1,0:T(8,128)(2,1)}, ...) | async-done | bytes 1572880 | tf_op jit(solution)/shard_map/psum | solution.py:328
  (757 shorter events, 519.5 us)
Async XLA Ops:
  7.2 27.3 %all-gather.4.cloned.1.call-start = ((), (), s32[]{:S(2)}) async-start(), calls=%async_computation.5 | async-start | bytes 1966080 | tf_op jit(solution)/shard_map/all_gather | solution.py:261
  7.9 51.0 %all-gather.6.cloned.1.call-start = ((), (), s32[]{:S(2)}) async-start(), calls=%async_computation.6 | async-start | bytes 2621440 | tf_op jit(solution)/shard_map/all_gather | solution.py:263
  8.6 74.5 %all-gather.8.cloned.1.call-start = ((), (), s32[]{:S(2)}) async-start(), calls=%async_computation.7 | async-start | bytes 2621440 | tf_op jit(solution)/shard_map/all_gather | solution.py:264
  9.4 666.3 %reduce-scatter.8.cloned.1.call-start = ((), (), s32[]{:S(2)}) async-start(), calls=%async_computation.9 | async-start | bytes 655360 | tf_op jit(solution)/shard_map/reduce_scatter | solution.py:314
  16.0 68.6 %copy-start.34 = (bf16[32,512]{1,0:T(8,128)(2,1)}, bf16[32,512]{1,0:T(8,128)(2,1)S(1)}, u32[]{:S(2)}) copy-start(bf16[32,512]{1,0:T(8,128)(2,1)S(1)} %all_gather.20) | copy-start | bytes 98308
  84.6 195.4 %copy-start.33 = (f32[20,512]{1,0:T(8,128)S(1)}, f32[20,512]{1,0:T(8,128)}, u32[]{:S(2)}) copy-start(f32[20,512]{1,0:T(8,128)} %custom-call.4) | copy-start | bytes 122884
  84.6 195.4 %copy-start.40 = (f32[2048]{0:T(1024)S(1)}, f32[2048]{0:T(1024)}, u32[]{:S(2)}) copy-start(f32[2048]{0:T(1024)} %custom-call.8) | copy-start | bytes 24580
  101.6 49.3 %copy-start.75 = (f32[512]{0:T(512)S(1)}, f32[512]{0:T(512)}, u32[]{:S(2)}) copy-start(f32[512]{0:T(512)} %get-tuple-element.1459) | copy-start | bytes 6148 | tf_op jit(solution)/shard_map/while
  198.6 49.3 %copy-start.75 = (f32[512]{0:T(512)S(1)}, f32[512]{0:T(512)}, u32[]{:S(2)}) copy-start(f32[512]{0:T(512)} %get-tuple-element.1459) | copy-start | bytes 6148 | tf_op jit(solution)/shard_map/while
  313.2 8.5 copy-start.6
  452.3 8.0 copy-start.43
  452.3 8.0 copy-start.46
  467.6 7.6 copy-start.54
  467.6 7.7 copy-start.57
  488.1 8.4 copy-start.6
  627.1 9.0 copy-start.43
  627.2 9.0 copy-start.46
  643.5 7.6 copy-start.54
  643.5 7.7 copy-start.57
  653.8 52.6 %reduce-scatter.6.cloned.1.call-start = ((), (), s32[]{:S(2)}) async-start(), calls=%async_computation.8 | async-start | bytes 1966080 | tf_op jit(solution)/shard_map/reduce_scatter | solution.py:311
  657.1 83.1 %reduce-scatter.10.cloned.1.call-start = ((), (), s32[]{:S(2)}) async-start(), calls=%async_computation.10 | async-start | bytes 2621440 | tf_op jit(solution)/shard_map/reduce_scatter | solution.py:317
  661.0 113.4 %reduce-scatter.12.cloned.1.call-start = ((), (), s32[]{:S(2)}) async-start(), calls=%async_computation.11 | async-start | bytes 2621440 | tf_op jit(solution)/shard_map/reduce_scatter | solution.py:320
  665.0 131.8 %reduce-scatter.14.cloned.1.call-start = ((), (), s32[]{:S(2)}) async-start(), calls=%async_computation.12 | async-start | bytes 40960 | tf_op jit(solution)/shard_map/reduce_scatter | solution.py:323
  670.5 220.9 %all-reduce.4.cloned.1.call-start = ((), (), s32[]{:S(2)}) async-start(), calls=%async_computation.13 | async-start | bytes 3145728 | tf_op jit(solution)/shard_map/psum | solution.py:328
  (138 other events, 459.5 us)
Sparse Core Ops, SparseCore 0:
  9.6 24.8 all-gather.3
  36.0 22.8 all-gather.5
  60.5 22.5 all-gather.7
  653.9 21.6 reduce-scatter.7
  678.2 28.1 reduce-scatter.5
  708.8 31.4 reduce-scatter.9
  742.9 31.4 reduce-scatter.11
  777.4 19.3 reduce-scatter.13
  801.1 90.2 all-reduce.3
where the time goes:
time: 923 us; the launch traced here: 904 us
  matrix products  332 us (36%)
  waiting for transfers between devices  254 us (28%)
  local copies, waits for them, and re-layouts  142 us (15%)
  other arithmetic  93.1 us (10%)
  blocking collectives  41.3 us (4%)
  loops' own time  27 us (3%)
  between operations  14.6 us (2%)
    psum x1, waiting for transfers between devices, body(): lax.psum(pieces[0].astype(jnp.bfloat16), 'rep').astype(jnp.float32)  71.6 us
    while x282, local copies, waits for them, and re-layouts  51.5 us
    dot_general x16, matrix products, attend(): jnp.dot(soft_rows, value_head, preferred_element_type=jnp.float32)  48.9 us
    dot_general x32, matrix products, head_scores(): jnp.einsum('qd,kd->qk', query_head, key_head, preferred_element_type=jnp....  45.2 us
    dot_general x16, matrix products, attend_back(): jnp.einsum('qk,qd->kd', grad_scores, query_head, preferred_element_type=j...  38.7 us
    dot_general x16, matrix products, attend_back(): jnp.einsum('qk,qd->kd', probs.astype(jnp.bfloat16), grad_head, preferred_...  37.7 us
    dynamic_slice x12, local copies, waits for them, and re-layouts, body(): lax.scan(partial(backward_one, weights_back), initial, (inputs, lengths,...  35.8 us
    reduce_scatter x1, waiting for transfers between devices, body(): lax.psum_scatter(totals[3].astype(jnp.bfloat16), 'shard', scatter_dimensi...  34.2 us
  transfers between devices with their start and end apart: 9, of which 9 were waited for; matrix products, arithmetic and copies ran while one was open for 2% of the time, Pallas kernels for 0%

commit v1 on v0

v1 whole, which is shorter than its diff:
```python
import math
from functools import partial

import jax
import jax.numpy as jnp
from jax import lax
from jax.experimental import pallas as pl
from jax.experimental.pallas import tpu as pltpu
from jax.sharding import PartitionSpec as P

D = 512
HEADS = 8
HDIM = 64
FF = 2048
MEM = 20
TILE = 256
PAIRS = HEADS // 2
SCALE = HDIM**-0.5
QSCALE = SCALE * math.log2(math.e)
LN2 = math.log(2.0)
F32 = jnp.float32
BF16 = jnp.bfloat16
VROWS = 80
VMEM_LIMIT = 62 * 2**20


def nn(a, b):
    return lax.dot_general(a, b, (((1,), (0,)), ((), ())), preferred_element_type=F32)


def nt(a, b):
    return lax.dot_general(a, b, (((1,), (1,)), ((), ())), preferred_element_type=F32)


def tn(a, b):
    return lax.dot_general(a, b, (((0,), (0,)), ((), ())), preferred_element_type=F32)


def key_sizes(seq_rows):
    top = -(-(seq_rows + MEM) // 32) * 32
    return [rows for rows in range(384, top, 128)] + [top]


def cdiv(a, b):
    return (a + b - 1) // b


def joined_rows(x_ref, memory, length, chunk, seq_rows):
    start = chunk * TILE
    row = lax.broadcasted_iota(jnp.int32, (TILE, 1), 0) + start
    pick = (
        lax.broadcasted_iota(jnp.int32, (TILE, 32), 0)
        + (start - length)
        == lax.broadcasted_iota(jnp.int32, (TILE, 32), 1)
    )
    placed = nn(jnp.where(pick, 1.0, 0.0).astype(BF16), memory)
    at = pl.multiple_of(jnp.minimum(start, seq_rows - TILE), TILE)
    tokens = x_ref[pl.ds(at, TILE), :].astype(F32)
    return jnp.where(row < length, tokens, placed).astype(BF16)


def fwd_kernel(
    seq_rows, len_ref, x_ref, w_ref, vec_ref, e_hbm, qt_ref, mixt_ref, inv_ref,
    wqt, wvt, keys, vt, qpad, ebuf, sems,
):
    length = len_ref[0]
    total = length + MEM
    sizes = key_sizes(seq_rows)
    memory = jnp.where(
        lax.broadcasted_iota(jnp.int32, (32, D), 0) < MEM, vec_ref[...].astype(F32), 0.0
    ).astype(BF16)
    vec_cols = vec_ref[...].astype(F32).T
    bias_q = vec_cols[:, MEM : MEM + 1]
    bias_v = vec_cols[:, MEM + 1 : MEM + 2]
    wqt[...] = w_ref[:, :D].T
    wvt[...] = w_ref[:, 2 * D :].T
    mixt_ref[...] = jnp.zeros(mixt_ref.shape, BF16)
    inv_ref[...] = jnp.zeros(inv_ref.shape, F32)
    qpad[...] = jnp.zeros(qpad.shape, BF16)
    vt[:, HDIM:, :] = jnp.ones((HEADS, VROWS - HDIM, vt.shape[2]), BF16)

    def project(chunk, _):
        rows = joined_rows(x_ref, memory, length, chunk, seq_rows)
        at = pl.multiple_of(chunk * TILE, TILE)
        here = pl.ds(at, TILE)
        key_rows = nn(rows, w_ref[:, D : 2 * D]).astype(BF16)
        for pair in range(PAIRS):
            keys[pair, here, :] = key_rows[:, pair * 128 : pair * 128 + 128]
        values = (nt(wvt[...], rows) + bias_v).astype(BF16)
        for head in range(HEADS):
            vt[head, :HDIM, here] = values[head * HDIM : (head + 1) * HDIM]

        @pl.when(at < seq_rows)
        def _():
            queries = ((nt(wqt[...], rows) + bias_q) * QSCALE).astype(BF16)
            qt_ref[:, here] = queries
            for head in range(HEADS):
                low = (head % 2) * HDIM
                qpad[head, low : low + HDIM, here] = queries[head * HDIM : (head + 1) * HDIM]

        return 0

    lax.fori_loop(0, cdiv(total, TILE), project, 0)
    n_tiles = cdiv(length, TILE)

    def attend(kr):
        tail = kr - 128 if kr % 128 == 0 else kr - kr % 128
        row = lax.broadcasted_iota(jnp.int32, (kr - tail, TILE), 0) + tail
        mask = row < total

        def copies(unit, slot):
            tile, pair = unit // PAIRS, unit % PAIRS
            return pltpu.make_async_copy(
                ebuf.at[slot, :, pl.ds(0, kr), :],
                e_hbm.at[tile, pl.ds(pair * 2, 2), pl.ds(0, kr), :],
                sems.at[slot],
            )

        def step(unit, _):
            slot = unit % 2
            tile, pair = unit // PAIRS, unit % PAIRS
            here = pl.ds(pl.multiple_of(tile * TILE, TILE), TILE)

            @pl.when(unit >= 2)
            def _():
                copies(unit - 2, slot).wait()

            slab = keys[pair, :kr, :]
            for sub in range(2):
                head = pair * 2 + sub
                scores = nn(slab, qpad[head, :, here])
                scores = jnp.concatenate(
                    [scores[:tail], jnp.where(mask, scores[tail:], -1e30)], 0
                )
                top = jnp.max(scores, axis=0, keepdims=True)
                expo = jnp.exp2(scores - top).astype(BF16)
                ebuf[slot, sub, :kr, :] = expo
                mixed = nn(vt[head, :, :kr], expo)
                inverse = 1.0 / mixed[HDIM : HDIM + 1]
                mixt_ref[pl.ds(pl.multiple_of(head * HDIM, HDIM), HDIM), here] = (
                    mixed[:HDIM] * inverse
                ).astype(BF16)
                inv_ref[pl.ds(head, 1), here] = inverse
            copies(unit, slot).start()
            return 0

        units = n_tiles * PAIRS
        lax.fori_loop(0, units, step, 0)
        copies(units - 2, units % 2).wait()
        copies(units - 1, (units - 1) % 2).wait()

    for index, kr in enumerate(sizes):
        least = sizes[index - 1] if index else 0

        @pl.when(jnp.logical_and(total > least, total <= kr))
        def _():
            attend(kr)


def attention_forward(length, x, w_qkv, vectors):
    seq_rows = x.shape[0]
    top = key_sizes(seq_rows)[-1]
    padded = cdiv(seq_rows + MEM, TILE) * TILE
    tiles = seq_rows // TILE
    vm = pl.BlockSpec(memory_space=pltpu.VMEM)
    return pl.pallas_call(
        partial(fwd_kernel, seq_rows),
        out_shape=(
            jax.ShapeDtypeStruct((tiles, HEADS, top, TILE), BF16),
            jax.ShapeDtypeStruct((D, seq_rows), BF16),
            jax.ShapeDtypeStruct((D, seq_rows), BF16),
            jax.ShapeDtypeStruct((HEADS, seq_rows), F32),
        ),
        in_specs=[pl.BlockSpec(memory_space=pltpu.SMEM), vm, vm, vm],
        out_specs=(pl.BlockSpec(memory_space=pl.ANY), vm, vm, vm),
        scratch_shapes=[
            pltpu.VMEM((D, D), BF16),
            pltpu.VMEM((D, D), BF16),
            pltpu.VMEM((PAIRS, padded, 128), BF16),
            pltpu.VMEM((HEADS, VROWS, padded), BF16),
            pltpu.VMEM((HEADS, 128, seq_rows), BF16),
            pltpu.VMEM((2, 2, top, TILE), BF16),
            pltpu.SemaphoreType.DMA((2,)),
        ],
        compiler_params=pltpu.CompilerParams(vmem_limit_bytes=VMEM_LIMIT),
        cost_estimate=pl.CostEstimate(
            flops=8 * 10**9, bytes_accessed=24 * 10**6, transcendentals=8 * 10**6
        ),
        name="attention_forward",
    )(length, x, w_qkv, vectors)


def norm_forward(values):
    center = values - jnp.mean(values, axis=-1, keepdims=True)
    inverse = lax.rsqrt(jnp.mean(center * center, axis=-1, keepdims=True) + 1e-05)
    return center * inverse, inverse


def norm_backward(grad, normed, inverse):
    return inverse * (
        grad
        - jnp.mean(grad, axis=-1, keepdims=True)
        - normed * jnp.mean(grad * normed, axis=-1, keepdims=True)
    )


def col_sum(values):
    return jnp.sum(values, axis=0, keepdims=True)


GELU_A = math.sqrt(2.0 / math.pi)
GELU_B = GELU_A * 0.044715
BLOCKS = FF // D


def ffn_kernel(
    seq_rows, len_ref, x_ref, cot_ref, mixt_ref, inv_ref, wo_ref, wi_ref, wb_ref, vec_ref,
    out_ref, gh_ref, dot_ref, gwo_ref, gwi_ref, gwb_ref, sums_ref,
    acc_o, acc_i, acc_b, slopes, actives,
):
    half = TILE // 2
    len0, len1 = len_ref[0], len_ref[1]
    n0, n1 = cdiv(len0, half), cdiv(len1, half)
    full = seq_rows // half
    n_all = n0 + n1
    out_ref[...] = jnp.zeros(out_ref.shape, BF16)
    gh_ref[...] = jnp.zeros(gh_ref.shape, F32)
    dot_ref[...] = jnp.zeros(dot_ref.shape, BF16)
    acc_o[...] = jnp.zeros(acc_o.shape, F32)
    acc_i[...] = jnp.zeros(acc_i.shape, F32)
    acc_b[...] = jnp.zeros(acc_b.shape, F32)
    sums_ref[...] = jnp.zeros(sums_ref.shape, F32)

    def vec(index):
        return vec_ref[index : index + 1, :].astype(F32)

    bias_out = vec(MEM + 2)
    bias_back = vec(MEM + 3 + BLOCKS)
    gain_one = vec(MEM + 4 + BLOCKS)
    shift_one = vec(MEM + 5 + BLOCKS)
    gain_two = vec(MEM + 6 + BLOCKS)
    shift_two = vec(MEM + 7 + BLOCKS)

    def place(chunk):
        second = chunk >= n0
        inside = jnp.where(second, chunk - n0, chunk)
        spare = chunk >= n_all
        seq = jnp.where(spare, jnp.where(n1 < full, 1, 0), jnp.where(second, 1, 0))
        inside = jnp.where(spare, jnp.where(n1 < full, n1, n0), inside)
        return seq, pl.multiple_of(inside * half, half), jnp.where(seq == 1, len1, len0)

    def step(index, _):
        spots = [place(index * 2), place(index * 2 + 1)]

        def rows_of(ref):
            return jnp.concatenate([ref[s, pl.ds(r, half), :] for s, r, _ in spots], 0)

        def lanes_of(ref):
            return jnp.concatenate([ref[s, :, pl.ds(r, half)] for s, r, _ in spots], 1)

        def put_rows(ref, value):
            for i, (s, r, _) in enumerate(spots):
                ref[s, pl.ds(r, half), :] = value[i * half : (i + 1) * half]

        def put_lanes(ref, value):
            for i, (s, r, _) in enumerate(spots):
                ref[s, :, pl.ds(r, half)] = value[:, i * half : (i + 1) * half]

        iota = lax.broadcasted_iota(jnp.int32, (half, 1), 0)
        valid = jnp.concatenate(
            [jnp.where(iota + r < count, 1.0, 0.0) for _, r, count in spots], 0
        )
        mixt = lanes_of(mixt_ref)
        attn = nn(mixt.T, wo_ref[...]) + bias_out
        normed_one, inverse_one = norm_forward(rows_of(x_ref).astype(F32) + attn)
        first = normed_one * gain_one + shift_one
        first_low = first.astype(BF16)
        second = first + bias_back
        for j in range(BLOCKS):
            cols = slice(j * D, (j + 1) * D)
            up = nn(first_low, wi_ref[:, cols]) + vec(MEM + 3 + j)
            square = up * up
            half_gate = 0.5 + 0.5 * jnp.tanh(up * (GELU_A + GELU_B * square))
            active = up * half_gate
            slopes[:, cols] = half_gate + active * (2.0 - 2.0 * half_gate) * (
                GELU_A + 3.0 * GELU_B * square
            )
            actives[:, cols] = active.astype(BF16)
            second = second + nn(active.astype(BF16), wb_ref[cols, :])
        normed_two, inverse_two = norm_forward(second)
        put_rows(out_ref, ((normed_two * gain_two + shift_two) * valid).astype(BF16))
        grad_out = rows_of(cot_ref).astype(F32) * valid
        sums_ref[MEM + 6 + BLOCKS : MEM + 7 + BLOCKS] += col_sum(grad_out * normed_two)
        sums_ref[MEM + 7 + BLOCKS : MEM + 8 + BLOCKS] += col_sum(grad_out)
        grad_second = norm_backward(grad_out * gain_two, normed_two, inverse_two)
        grad_down = grad_second.astype(BF16)
        sums_ref[MEM + 3 + BLOCKS : MEM + 4 + BLOCKS] += col_sum(grad_down.astype(F32))
        grad_first = grad_second
        first_t = first_low.T
        for j in range(BLOCKS):
            cols = slice(j * D, (j + 1) * D)
            acc_b[cols, :] += tn(actives[:, cols], grad_down)
            grad_up = (nt(grad_down, wb_ref[cols, :]) * slopes[:, cols]).astype(BF16)
            sums_ref[MEM + 3 + j : MEM + 4 + j] += col_sum(grad_up.astype(F32))
            acc_i[:, cols] += nn(first_t, grad_up)
            grad_first = grad_first + nt(grad_up, wi_ref[:, cols])
        sums_ref[MEM + 4 + BLOCKS : MEM + 5 + BLOCKS] += col_sum(grad_first * normed_one)
        sums_ref[MEM + 5 + BLOCKS : MEM + 6 + BLOCKS] += col_sum(grad_first)
        grad_one = norm_backward(grad_first * gain_one, normed_one, inverse_one)
        put_rows(gh_ref, grad_one)
        grad_attn = grad_one.astype(BF16)
        sums_ref[MEM + 2 : MEM + 3] += col_sum(grad_attn.astype(F32))
        acc_o[...] += nn(mixt, grad_attn)
        grad_mixed = nt(wo_ref[...], grad_attn)
        inverse = lanes_of(inv_ref)
        scaled = jnp.concatenate(
            [
                grad_mixed[h * HDIM : (h + 1) * HDIM] * inverse[h : h + 1]
                for h in range(HEADS)
            ],
            0,
        )
        put_lanes(dot_ref, scaled.astype(BF16))
        return 0

    lax.fori_loop(0, cdiv(n_all, 2), step, 0)
    gwo_ref[...] = acc_o[...].astype(BF16)
    gwi_ref[...] = acc_i[...].astype(BF16)
    gwb_ref[...] = acc_b[...].astype(BF16)


def feed_forward(lengths, x, cot, mixt, inv, w_out, w_in, w_back, vectors):
    count, seq_rows = x.shape[:2]
    vm = pl.BlockSpec(memory_space=pltpu.VMEM)
    return pl.pallas_call(
        partial(ffn_kernel, seq_rows),
        out_shape=(
            jax.ShapeDtypeStruct((count, seq_rows, D), BF16),
            jax.ShapeDtypeStruct((count, seq_rows, D), F32),
            jax.ShapeDtypeStruct((count, D, seq_rows), BF16),
            jax.ShapeDtypeStruct((D, D), BF16),
            jax.ShapeDtypeStruct((D, FF), BF16),
            jax.ShapeDtypeStruct((FF, D), BF16),
            jax.ShapeDtypeStruct((32, D), F32),
        ),
        in_specs=[pl.BlockSpec(memory_space=pltpu.SMEM)] + [vm] * 8,
        out_specs=(vm,) * 7,
        scratch_shapes=[
            pltpu.VMEM((D, D), F32),
            pltpu.VMEM((D, FF), F32),
            pltpu.VMEM((FF, D), F32),
            pltpu.VMEM((TILE, FF), F32),
            pltpu.VMEM((TILE, FF), BF16),
        ],
        compiler_params=pltpu.CompilerParams(vmem_limit_bytes=VMEM_LIMIT),
        cost_estimate=pl.CostEstimate(
            flops=27 * 10**9, bytes_accessed=24 * 10**6, transcendentals=4 * 10**6
        ),
        name="feed_forward",
    )(lengths, x, cot, mixt, inv, w_out, w_in, w_back, vectors)


def bwd_kernel(
    seq_rows, groups, group, n_seqs, *refs,
):
    gp = PAIRS // groups
    gcols = gp * 128
    len_ref, x_ref, w_ref, vec_ref, qt_ref, mixt_ref, dot_ref = refs[:7]
    e_refs = refs[7 : 7 + n_seqs]
    dw_ref, proj_ref, sums_ref = refs[7 + n_seqs : 10 + n_seqs]
    wkt, kt, values, qpad, dpad, dqt, dk, dv, ebuf, acc, sems = refs[10 + n_seqs :]
    sizes = key_sizes(seq_rows)
    base = group * gcols
    memory = jnp.where(
        lax.broadcasted_iota(jnp.int32, (32, D), 0) < MEM, vec_ref[...].astype(F32), 0.0
    ).astype(BF16)
    bias_v = vec_ref[MEM + 1 : MEM + 2, base : base + gcols].astype(F32)
    wkt[...] = w_ref[:, D + base : D + base + gcols].T
    acc[...] = jnp.zeros(acc.shape, F32)
    proj_ref[...] = jnp.zeros(proj_ref.shape, BF16)
    sums_ref[...] = jnp.zeros(sums_ref.shape, F32)
    qpad[...] = jnp.zeros(qpad.shape, BF16)
    dpad[...] = jnp.zeros(dpad.shape, BF16)

    for seq in range(n_seqs):
        length = len_ref[seq]
        total = length + MEM
        chunks = cdiv(total, TILE)
        n_tiles = cdiv(length, TILE)
        e_hbm = e_refs[seq]

        def project(chunk, _):
            rows = joined_rows(x_ref.at[seq], memory, length, chunk, seq_rows)
            here = pl.ds(pl.multiple_of(chunk * TILE, TILE), TILE)
            value_rows = (
                nn(rows, w_ref[:, 2 * D + base : 2 * D + base + gcols]) + bias_v
            ).astype(BF16)
            for pair in range(gp):
                values[pair, here, :] = value_rows[:, pair * 128 : pair * 128 + 128]
            kt[:, here] = nt(wkt[...], rows).astype(BF16)
            dqt[:, here] = jnp.zeros((gcols, TILE), BF16)
            for pair in range(gp):
                dk[pair, here, :] = jnp.zeros((TILE, 128), F32)
                dv[pair, here, :] = jnp.zeros((TILE, 128), F32)
            return 0

        lax.fori_loop(0, chunks, project, 0)

        def attend(kr):
            def copies(unit, slot):
                pair, tile = unit // n_tiles, unit % n_tiles
                return pltpu.make_async_copy(
                    e_hbm.at[tile, pl.ds((group * gp + pair) * 2, 2), pl.ds(0, kr), :],
                    ebuf.at[slot, :, pl.ds(0, kr), :],
                    sems.at[slot],
                )

            units = n_tiles * gp
            copies(0, 0).start()

            def step(unit, _):
                slot = unit % 2
                pair, tile = unit // n_tiles, unit % n_tiles
                here = pl.ds(pl.multiple_of(tile * TILE, TILE), TILE)

                @pl.when(unit + 1 < units)
                def _():
                    copies(unit + 1, (unit + 1) % 2).start()

                copies(unit, slot).wait()
                slab = values[pair, :kr, :]
                grads, expos = [], []
                for sub in range(2):
                    low = sub * HDIM
                    local = pl.ds(pl.multiple_of(pair * 128 + low, HDIM), HDIM)
                    spot = pl.ds(pl.multiple_of(base + pair * 128 + low, HDIM), HDIM)
                    outer = dot_ref[seq, spot, here]
                    dpad[sub, low : low + HDIM, :] = outer
                    qpad[sub, low : low + HDIM, :] = qt_ref[seq, spot, here]
                    inner = col_sum(
                        outer.astype(F32) * mixt_ref[seq, spot, here].astype(F32)
                    )
                    expo = ebuf[slot, sub, :kr, :]
                    grad = (
                        expo.astype(F32) * (nn(slab, dpad[sub]) - inner)
                    ).astype(BF16)
                    dqt[local, here] = (nn(kt[local, :kr], grad) * SCALE).astype(BF16)
                    grads.append(grad)
                    expos.append(expo)
                dk[pair, :kr, :] += nt(
                    jnp.concatenate(grads, 1), jnp.concatenate([qpad[0], qpad[1]], 1)
                )
                dv[pair, :kr, :] += nt(
                    jnp.concatenate(expos, 1), jnp.concatenate([dpad[0], dpad[1]], 1)
                )
                return 0

            lax.fori_loop(0, units, step, 0)

        for index, kr in enumerate(sizes):
            least = sizes[index - 1] if index else 0

            @pl.when(jnp.logical_and(total > least, total <= kr))
            def _():
                attend(kr)

        def finish(chunk, _):
            rows = joined_rows(x_ref.at[seq], memory, length, chunk, seq_rows)
            here = pl.ds(pl.multiple_of(chunk * TILE, TILE), TILE)
            parts = [dqt[:, here].T]
            parts += [(dk[pair, here, :] * LN2).astype(BF16) for pair in range(gp)]
            parts += [dv[pair, here, :].astype(BF16) for pair in range(gp)]
            grad = jnp.concatenate(parts, 1)
            proj_ref[seq, here, :] = grad
            acc[...] += tn(rows, grad)
            sums_ref[0:1, :] += col_sum(grad.astype(F32))
            return 0

        lax.fori_loop(0, chunks, finish, 0)

    dw_ref[...] = acc[...].astype(BF16)


def attention_backward(group, groups, lengths, x, w_qkv, vectors, qt, mixt, dot, expos):
    count, seq_rows = x.shape[:2]
    top = key_sizes(seq_rows)[-1]
    padded = cdiv(seq_rows + MEM, TILE) * TILE
    gp = PAIRS // groups
    gcols = gp * 128
    vm = pl.BlockSpec(memory_space=pltpu.VMEM)
    return pl.pallas_call(
        partial(bwd_kernel, seq_rows, groups, group, count),
        out_shape=(
            jax.ShapeDtypeStruct((D, 3 * gcols), BF16),
            jax.ShapeDtypeStruct((count, padded, 3 * gcols), BF16),
            jax.ShapeDtypeStruct((8, 3 * gcols), F32),
        ),
        in_specs=[pl.BlockSpec(memory_space=pltpu.SMEM)]
        + [vm] * 6
        + [pl.BlockSpec(memory_space=pl.ANY)] * count,
        out_specs=(vm, vm, vm),
        scratch_shapes=[
            pltpu.VMEM((gcols, D), BF16),
            pltpu.VMEM((gcols, padded), BF16),
            pltpu.VMEM((gp, padded, 128), BF16),
            pltpu.VMEM((2, 128, TILE), BF16),
            pltpu.VMEM((2, 128, TILE), BF16),
            pltpu.VMEM((gcols, padded), BF16),
            pltpu.VMEM((gp, padded, 128), F32),
            pltpu.VMEM((gp, padded, 128), F32),
            pltpu.VMEM((2, 2, top, TILE), BF16),
            pltpu.VMEM((D, 3 * gcols), F32),
            pltpu.SemaphoreType.DMA((2,)),
        ],
        compiler_params=pltpu.CompilerParams(vmem_limit_bytes=VMEM_LIMIT),
        cost_estimate=pl.CostEstimate(
            flops=16 * 10**9, bytes_accessed=30 * 10**6, transcendentals=0
        ),
        name="attention_backward",
    )(lengths, x, w_qkv, vectors, qt, mixt, dot, *expos)


def input_kernel(seq_rows, groups, len_ref, w_ref, gh_ref, *refs):
    projs = refs[:groups]
    gx_ref, mem_ref = refs[groups:]
    gcols = D // groups
    gx_ref[...] = jnp.zeros(gx_ref.shape, BF16)
    mem_ref[...] = jnp.zeros(mem_ref.shape, F32)

    def joint(seq, here):
        parts = [
            projs[g][seq, here, kind * gcols : (kind + 1) * gcols]
            for kind in range(3)
            for g in range(groups)
        ]
        return jnp.concatenate(parts, 1)

    for seq in range(gx_ref.shape[0]):
        length = len_ref[seq]

        def step(chunk, _):
            start = pl.multiple_of(chunk * TILE, TILE)
            here = pl.ds(start, TILE)
            grad = nt(joint(seq, here), w_ref[...])
            row = lax.broadcasted_iota(jnp.int32, (TILE, 1), 0) + start

            @pl.when(start < seq_rows)
            def _():
                gx_ref[seq, here, :] = jnp.where(
                    row < length, grad + gh_ref[seq, pl.ds(start, TILE), :], 0.0
                ).astype(BF16)

            @pl.when(start + TILE > length)
            def _():
                pick = (
                    lax.broadcasted_iota(jnp.int32, (32, TILE), 1) + (start - length)
                    == lax.broadcasted_iota(jnp.int32, (32, TILE), 0)
                )
                pick = jnp.logical_and(pick, lax.broadcasted_iota(jnp.int32, (32, TILE), 0) < MEM)
                mem_ref[...] += nn(jnp.where(pick, 1.0, 0.0).astype(BF16), grad.astype(BF16))

            return 0

        lax.fori_loop(0, cdiv(length + MEM, TILE), step, 0)


def input_gradient(lengths, w_qkv, gh, projs):
    count, seq_rows = gh.shape[:2]
    vm = pl.BlockSpec(memory_space=pltpu.VMEM)
    return pl.pallas_call(
        partial(input_kernel, seq_rows, len(projs)),
        out_shape=(
            jax.ShapeDtypeStruct((count, seq_rows, D), BF16),
            jax.ShapeDtypeStruct((32, D), F32),
        ),
        in_specs=[pl.BlockSpec(memory_space=pltpu.SMEM)] + [vm] * (2 + len(projs)),
        out_specs=(vm, vm),
        compiler_params=pltpu.CompilerParams(vmem_limit_bytes=VMEM_LIMIT),
        cost_estimate=pl.CostEstimate(
            flops=3 * 10**9, bytes_accessed=14 * 10**6, transcendentals=0
        ),
        name="input_gradient",
    )(lengths, w_qkv, gh, *projs)


GROUPS = 2


def local_layer(lengths, x, w_qkv, w_out, w_in, w_back, vectors, cot):
    count = x.shape[0]
    fwd = [
        attention_forward(lax.slice(lengths, (s,), (s + 1,)), x[s], w_qkv, vectors)
        for s in range(count)
    ]
    qt = jnp.stack([f[1] for f in fwd])
    mixt = jnp.stack([f[2] for f in fwd])
    inv = jnp.stack([f[3] for f in fwd])
    out, gh, dot, gwo, gwi, gwb, sums = feed_forward(
        lengths, x, cot, mixt, inv, w_out, w_in, w_back, vectors
    )
    back = [
        attention_backward(
            g, GROUPS, lengths, x, w_qkv, vectors, qt, mixt, dot, [f[0] for f in fwd]
        )
        for g in range(GROUPS)
    ]
    gx, mem = input_gradient(lengths, w_qkv, gh, [b[1] for b in back])
    gcols = D // GROUPS
    dw = jnp.concatenate(
        [b[0][:, k * gcols : (k + 1) * gcols] for k in range(3) for b in back], 1
    )
    psum = jnp.concatenate(
        [b[2][0, k * gcols : (k + 1) * gcols] for k in range(3) for b in back], 0
    )
    rows = sums.at[:MEM].set(mem[:MEM]).at[MEM].set(psum[:D]).at[MEM + 1].set(psum[2 * D :])
    return out, gx, dw, gwo, gwi, gwb, rows


def bits_of(size):
    bit, bits = size // 2, []
    while bit:
        bits.append(bit)
        bit //= 2
    return bits


def exchange(value, axis, size, bit):
    return lax.ppermute(value, axis, [(i, i ^ bit) for i in range(size)])


def gather_pieces(value, axis, size):
    pieces = {0: value}
    for bit in bits_of(size):
        for mask in sorted(pieces):
            pieces[mask | bit] = exchange(pieces[mask], axis, size, bit)
    return [pieces[mask] for mask in range(size)]


def gather_rows(value, axis, size):
    me = lax.axis_index(axis)
    rows = value.shape[0]
    whole = jnp.zeros((size * rows,) + value.shape[1:], value.dtype)
    for mask, piece in enumerate(gather_pieces(value, axis, size)):
        whole = lax.dynamic_update_slice_in_dim(whole, piece, (me ^ mask) * rows, 0)
    return whole


def add_low(a, b):
    return (a.astype(F32) + b.astype(F32)).astype(BF16)


def reduce_shard(blocks, axis, size):
    me = lax.axis_index(axis)
    parts = [lax.dynamic_index_in_dim(blocks, me ^ m, 0, False) for m in range(size)]
    live = {m: parts[m] for m in range(size)}
    bit = 1
    while bit < size:
        live = {
            m: add_low(live[m], exchange(live[m | bit], axis, size, bit))
            for m in live
            if not m & bit
        }
        bit *= 2
    return live[0]


def reduce_rep(value, axis, size):
    me = lax.axis_index(axis)
    steps = []
    bit = 1
    while bit < size:
        steps.append(bit)
        bit *= 2
    for bit in steps:
        half = value.shape[0] // 2
        high = (me & bit) != 0
        low_part, high_part = value[:half], value[half:]
        send = jnp.where(high, low_part, high_part)
        keep = jnp.where(high, high_part, low_part)
        value = add_low(keep, exchange(send, axis, size, bit))
    for bit in reversed(steps):
        high = (me & bit) != 0
        other = exchange(value, axis, size, bit)
        value = jnp.where(
            high, jnp.concatenate([other, value], 0), jnp.concatenate([value, other], 0)
        )
    return value


def body(sizes, inputs, lengths, w_qkv, w_out, w_in, w_back, vectors, cotangent):
    reps, shards = sizes
    full = [gather_rows(w, "shard", shards) for w in (w_qkv, w_out, w_in, w_back, vectors)]
    out, gx, dw, gwo, gwi, gwb, rows = local_layer(lengths, inputs, *full, cotangent)

    def split(grad):
        grad = grad.astype(BF16)
        grad = grad.reshape(shards, grad.shape[0] // shards, grad.shape[1])
        return grad.reshape(shards, -1, D)

    grads = (dw, gwo, gwi, gwb, rows)
    blocks = jnp.concatenate([split(g) for g in grads], 1)
    spare = -blocks.shape[1] % (16 * reps)
    blocks = jnp.pad(blocks, ((0, 0), (0, spare), (0, 0)))
    total = reduce_rep(reduce_shard(blocks, "shard", shards), "rep", reps).astype(F32)
    outs, at = [], 0
    for g in grads:
        count = g.size // shards // D
        outs.append(total[at : at + count].reshape(g.shape[0] // shards, g.shape[1]))
        at += count
    return (out, gx, *outs)


def solution(mesh):
    data = P(("rep", "shard"), None, None)
    rows = P("shard", None)
    return jax.shard_map(
        partial(body, (mesh.shape["rep"], mesh.shape["shard"])),
        mesh=mesh,
        in_specs=(data, P(("rep", "shard")), rows, rows, rows, rows, rows, data),
        out_specs=(data, data, rows, rows, rows, rows, rows),
        check_vma=False,
    )
```

time: 923 us -> 454 us (0.49); the launches traced: 904 us -> 447 us
  matrix products: 332 us -> 0 us
  Pallas kernels: 0 us -> 161 us
  waiting for transfers between devices: 254 us -> 142 us
  local copies, waits for them, and re-layouts: 142 us -> 50.6 us
  other arithmetic: 93.1 us -> 12.9 us
  starting transfers between devices: 0.36 us -> 79.4 us
  blocking collectives: 41.3 us -> 0 us
  loops' own time: 27 us -> 0 us
  between operations: 14.6 us -> 1.32 us
    dot_general x136 -> x0, matrix products: 332 us -> none  [the longest x16 48.9 us: attend(): jnp.dot(soft_rows, value_head, preferred_element_type=jnp.float32)]
    pallas_call x0 -> x6, Pallas kernels: none -> 161 us  [the longest x2 62.5 us: attention_backward(): pl.pallas_call(partial(bwd_kernel, seq_rows, groups, group, count), out_s...]
    ppermute x0 -> x24, waiting for transfers between devices: none -> 142 us  [exchange(): return lax.ppermute(value, axis, [(i, i ^ bit) for i in range(size)])]
    reduce_scatter x5 -> x0, waiting for transfers between devices: 126 us -> none  [the longest x1 34.2 us: body(): lax.psum_scatter(totals[3].astype(jnp.bfloat16), 'shard', scatter_dimensi...]
    ppermute x0 -> x24, starting transfers between devices: none -> 79.4 us  [exchange(): return lax.ppermute(value, axis, [(i, i ^ bit) for i in range(size)])]
    psum x1 -> x0, waiting for transfers between devices: 71.6 us -> none  [body(): lax.psum(pieces[0].astype(jnp.bfloat16), 'rep').astype(jnp.float32)]
    all_gather x3 -> x0, waiting for transfers between devices: 54.5 us -> none  [the longest x1 24.5 us: body(): lax.all_gather(w_in, 'shard', axis=0, tiled=True)]
    while x283 -> x0, local copies, waits for them, and re-layouts: 51.6 us -> none
  transfers between devices with their start and end apart: 9 -> 24, of which waited for: 9 -> 13; matrix products, arithmetic and copies ran while one was open for 2% -> 6% of each run, Pallas kernels for 0% -> 10%
where the time goes in v1:
time: 454 us; the launch traced here: 447 us
  Pallas kernels  161 us (35%)
  waiting for transfers between devices  142 us (31%)
  starting transfers between devices  79.4 us (17%)
  local copies, waits for them, and re-layouts  50.6 us (11%)
  other arithmetic  12.9 us (3%)
    ppermute x24, waiting for transfers between devices, exchange(): return lax.ppermute(value, axis, [(i, i ^ bit) for i in range(size)])  142 us
    ppermute x24, starting transfers between devices, exchange(): return lax.ppermute(value, axis, [(i, i ^ bit) for i in range(size)])  79.4 us
    pallas_call x2, Pallas kernels, attention_backward(): pl.pallas_call(partial(bwd_kernel, seq_rows, groups, group, count), out_s...  62.5 us
    pallas_call x2, Pallas kernels, attention_forward(): pl.pallas_call(partial(fwd_kernel, seq_rows), out_shape=(jax.ShapeDtypeSt...  44.3 us
    pallas_call x1, Pallas kernels, feed_forward(): pl.pallas_call(partial(ffn_kernel, seq_rows), out_shape=(jax.ShapeDtypeSt...  42.6 us
    dynamic_update_slice x20, local copies, waits for them, and re-layouts, gather_rows(): whole = lax.dynamic_update_slice_in_dim(whole, piece, (me ^ mask) * rows, 0)  14 us
    unnamed x45, local copies, waits for them, and re-layouts  12.8 us
    pallas_call x1, Pallas kernels, input_gradient(): pl.pallas_call(partial(input_kernel, seq_rows, len(projs)), out_shape=(ja...  11.5 us
  transfers between devices with their start and end apart: 24, of which 13 were waited for; matrix products, arithmetic and copies ran while one was open for 6% of the time, Pallas kernels for 10%

profile of v1, /device:TPU:0, one launch (start us, length us, event | category | flops | bytes accessed | tf_op | source)
XLA Modules:
  0.0 446.7 jit_solution(15106096146266621566)
XLA Ops:
  4.2 3.0 slice_bitcast_fusion.1
  25.7 6.9 %collective-permute-done.10 = bf16[128,2048]{1,0:T(8,128)(2,1)} collective-permute-done((bf16[128,2048]{1,0:T(8,128)(2,1)S(1)}, bf16[128,2048]{1,0:T(8,128)(2,1)}, u32[]{:S(2)}, u32[]{:S(2)}) %collective-permute-start.10) | collective-permute-done | bytes 524320 | tf_op jit(solution)/shard_map/ppermute | solution.py:628
  32.6 10.6 %collective-permute-done.13 = bf16[512,512]{1,0:T(8,128)(2,1)} collective-permute-done((bf16[512,512]{1,0:T(8,128)(2,1)}, bf16[512,512]{1,0:T(8,128)(2,1)}, u32[]{:S(2)}, u32[]{:S(2)}) %collective-permute-start.13) | collective-permute-done | bytes 524320 | tf_op jit(solution)/shard_map/ppermute | solution.py:628
  49.9 34.1 %attention_forward.2 = (bf16[4,8,1056,256]{3,2,1,0:T(8,128)(2,1)}, bf16[512,1024]{1,0:T(8,128)(2,1)}, bf16[512,1024]{1,0:T(8,128)(2,1)}, f32[8,1024]{1,0:T(8,128)}) custom-call(s32[1]{0:T(128)} %get-tuple-element.99.len_ref, bf16[1024,512]{1,0:T(8,128)(2,1)} %get-tuple-element.93.x_ref, bf16[512,1536]{1,0:T(8,128)(2,1)} %copy-done.1, bf16[32,512]{1,0:T(8,128)(2,1)} %copy-done.13), custom_call_target="tpu_custom_call" | custom-call | flops 8000000000 | bytes 24000000 | tf_op jit(solution)/shard_map/attention_forward/pallas_call | solution.py:166
  84.0 10.3 %attention_forward.3 = (bf16[4,8,1056,256]{3,2,1,0:T(8,128)(2,1)}, bf16[512,1024]{1,0:T(8,128)(2,1)}, bf16[512,1024]{1,0:T(8,128)(2,1)}, f32[8,1024]{1,0:T(8,128)}) custom-call(s32[1]{0:T(128)} %get-tuple-element.100.len_ref, bf16[1024,512]{1,0:T(8,128)(2,1)} %get-tuple-element.94.x_ref, bf16[512,1536]{1,0:T(8,128)(2,1)} %copy-done.1, bf16[32,512]{1,0:T(8,128)(2,1)} %copy-done.13), custom_call_target="tpu_custom_call" | custom-call | flops 8000000000 | bytes 24000000 | tf_op jit(solution)/shard_map/attention_forward/pallas_call | solution.py:166
  94.3 2.9 pad_maximum_fusion.mixt_ref.refs_5_
  103.1 42.6 %feed_forward.1 = (bf16[2,1024,512]{2,1,0:T(8,128)(2,1)}, f32[2,1024,512]{2,1,0:T(8,128)}, bf16[2,512,1024]{2,1,0:T(8,128)(2,1)}, bf16[512,512]{1,0:T(8,128)(2,1...) custom-call(s32[2]{0:T(128)} %len_ref.3, bf16[2,1024,512]{2,1,0:T(8,128)(2,1)} %refs_1_.3, ...), custom_call_target="tpu_custom_call" | custom-call | flops 27000000512 | bytes 24000000 | tf_op jit(solution)/shard_map/feed_forward/pallas_call | solution.py:335
  145.8 31.4 %attention_backward.3 = (bf16[512,768]{1,0:T(8,128)(2,1)}, bf16[2,1280,768]{2,1,0:T(8,128)(2,1)}, f32[8,768]{1,0:T(8,128)}) custom-call(s32[2]{0:T(128)} %len_ref.3, bf16[2,1024,512]{2,1,0:T(8,128)(2,1)} %refs_1_.3, bf16[512,1536]{1,0:T(8,128)(2,1)} %copy-done.1, bf16[32,512]{1,0:T(8,128)(2,1)} %copy-done.13, ...), custom_call_target="tpu_custom_call" | custom-call | flops 16000000000 | bytes 30000000 | tf_op jit(solution)/shard_map/attention_backward/pallas_call | solution.py:491
  177.2 31.1 %attention_backward.2 = (bf16[512,768]{1,0:T(8,128)(2,1)}, bf16[2,1280,768]{2,1,0:T(8,128)(2,1)}, f32[8,768]{1,0:T(8,128)}) custom-call(s32[2]{0:T(128)} %len_ref.3, bf16[2,1024,512]{2,1,0:T(8,128)(2,1)} %refs_1_.3, bf16[512,1536]{1,0:T(8,128)(2,1)} %copy-done.1, bf16[32,512]{1,0:T(8,128)(2,1)} %copy-done.13, ...), custom_call_target="tpu_custom_call" | custom-call | flops 16000000000 | bytes 30000000 | tf_op jit(solution)/shard_map/attention_backward/pallas_call | solution.py:491
  209.8 11.5 %input_gradient.1 = (bf16[2,1024,512]{2,1,0:T(8,128)(2,1)}, f32[32,512]{1,0:T(8,128)}) custom-call(s32[2]{0:T(128)} %len_ref.3, bf16[512,1536]{1,0:T(8,128)(2,1)} %copy-done.1, f32[2,1024,512]{2,1,0:T(8,128)} %get-tuple-element.71.gh_ref, bf16[2,1280,768]{2,1,0:T(8,128)(2,1)} %get-tuple-element.77.refs_0_, bf16[2,1280,768]{2,1,0:T(8,128)(2,1)} %get-tuple-element.78.refs_1_), custom_call_target="tpu_custom_call" | custom-call | flops 3000000000 | bytes 14000000 | tf_op jit(solution)/shard_map/input_gradient/pallas_call | solution.py:570
  230.0 3.2 reshape_reshape.7
  241.2 21.2 %collective-permute-start.16 = (bf16[1664,512]{1,0:T(8,128)(2,1)S(1)}, bf16[1664,512]{1,0:T(8,128)(2,1)}, u32[]{:S(2)}, u32[]{:S(2)}) collective-permute-start(bf16[1664,512]{1,0:T(8,128)(2,1)S(1)} %get-tuple-element.90), channel_id=1, source_target_pairs={{0,1},{1,0},{2,3},{3,2},{4,5},{5,4},{6,7},{7,6},{8,9},{9,8},{10,11... | collective-permute-start | bytes 5111816 | tf_op jit(solution)/shard_map/ppermute | solution.py:628
  262.5 3.3 collective-permute-done.16
  268.2 21.5 %collective-permute-start.17 = (bf16[1664,512]{1,0:T(8,128)(2,1)S(1)}, bf16[1664,512]{1,0:T(8,128)(2,1)}, u32[]{:S(2)}, u32[]{:S(2)}) collective-permute-start(bf16[1664,512]{1,0:T(8,128)(2,1)S(1)} %fusion), channel_id=1, source_target_pairs={{0,2},{1,3},{2,0},{3,1},{4,6},{5,7},{6,4},{7,5},{8,10},{9,11},{10,... | collective-permute-start | bytes 5111816 | tf_op jit(solution)/shard_map/ppermute | solution.py:628
  289.7 37.6 %collective-permute-done.17 = bf16[1664,512]{1,0:T(8,128)(2,1)} collective-permute-done((bf16[1664,512]{1,0:T(8,128)(2,1)S(1)}, bf16[1664,512]{1,0:T(8,128)(2,1)}, u32[]{:S(2)}, u32[]{:S(2)}) %collective-permute-start.17) | collective-permute-done | bytes 1703968 | tf_op jit(solution)/shard_map/ppermute | solution.py:628
  327.3 3.1 add_convert_fusion
  330.6 20.5 %collective-permute-done.18 = bf16[832,512]{1,0:T(8,128)(2,1)S(1)} collective-permute-done((bf16[832,512]{1,0:T(8,128)(2,1)S(1)}, bf16[832,512]{1,0:T(8,128)(2,1)S(1)}, u32[]{:S(2)}, u32[]{:S(2)}) %collective-permute-start.18) | collective-permute-done | bytes 852000 | tf_op jit(solution)/shard_map/ppermute | solution.py:628
  351.5 10.4 %collective-permute-done.19 = bf16[416,512]{1,0:T(8,128)(2,1)S(1)} collective-permute-done((bf16[416,512]{1,0:T(8,128)(2,1)S(1)}, bf16[416,512]{1,0:T(8,128)(2,1)S(1)}, u32[]{:S(2)}, u32[]{:S(2)}) %collective-permute-start.19) | collective-permute-done | bytes 426016 | tf_op jit(solution)/shard_map/ppermute | solution.py:628
  362.1 27.0 %collective-permute-start.20 = (bf16[208,512]{1,0:T(8,128)(2,1)S(1)}, bf16[208,512]{1,0:T(8,128)(2,1)S(1)}, u32[]{:S(2)}, u32[]{:S(2)}) collective-permute-start(bf16[208,512]{1,0:T(8,128)(2,1)S(1)} %broadcast_select_fusion.2), channel_id=1, source_target_pairs={{0,16},{4,20},{8,24},{12,28},{16,0},{20,4},{24,8},{28,12},{1,17},{... | collective-permute-start | bytes 638984 | tf_op jit(solution)/shard_map/ppermute | solution.py:628
  389.1 8.0 %collective-permute-done.20 = bf16[208,512]{1,0:T(8,128)(2,1)S(1)} collective-permute-done((bf16[208,512]{1,0:T(8,128)(2,1)S(1)}, bf16[208,512]{1,0:T(8,128)(2,1)S(1)}, u32[]{:S(2)}, u32[]{:S(2)}) %collective-permute-start.20) | collective-permute-done | bytes 213024 | tf_op jit(solution)/shard_map/ppermute | solution.py:628
  397.3 11.7 %collective-permute-done.21 = bf16[208,512]{1,0:T(8,128)(2,1)S(1)} collective-permute-done((bf16[208,512]{1,0:T(8,128)(2,1)S(1)}, bf16[208,512]{1,0:T(8,128)(2,1)S(1)}, u32[]{:S(2)}, u32[]{:S(2)}) %collective-permute-start.21) | collective-permute-done | bytes 213024 | tf_op jit(solution)/shard_map/ppermute | solution.py:628
  409.2 10.6 %collective-permute-done.22 = bf16[416,512]{1,0:T(8,128)(2,1)S(1)} collective-permute-done((bf16[416,512]{1,0:T(8,128)(2,1)S(1)}, bf16[416,512]{1,0:T(8,128)(2,1)S(1)}, u32[]{:S(2)}, u32[]{:S(2)}) %collective-permute-start.22) | collective-permute-done | bytes 426016 | tf_op jit(solution)/shard_map/ppermute | solution.py:628
  420.7 18.3 %collective-permute-done.23 = bf16[832,512]{1,0:T(8,128)(2,1)S(1)} collective-permute-done((bf16[832,512]{1,0:T(8,128)(2,1)S(1)}, bf16[832,512]{1,0:T(8,128)(2,1)S(1)}, u32[]{:S(2)}, u32[]{:S(2)}) %collective-permute-start.23) | collective-permute-done | bytes 852000 | tf_op jit(solution)/shard_map/ppermute | solution.py:628
  442.6 2.7 reshape.114
  (136 shorter events, 62.0 us)
Async XLA Ops:
  0.6 23.4 %collective-permute-start = (bf16[128,1536]{1,0:T(8,128)(2,1)}, bf16[128,1536]{1,0:T(8,128)(2,1)}, u32[]{:S(2)}, u32[]{:S(2)}) collective-permute-start(bf16[128,1536]{1,0:T(8,128)(2,1)} %param.16), channel_id=1, source_target_pairs={{0,1},{1,0},{2,3},{3,2},{4,5},{5,4},{6,7},{7,6},{8,9},{9,8},{10,11... | collective-permute-start | bytes 1179656 | tf_op jit(solution)/shard_map/ppermute | solution.py:628
  1.1 23.0 %collective-permute-start.1 = (bf16[128,1536]{1,0:T(8,128)(2,1)}, bf16[128,1536]{1,0:T(8,128)(2,1)S(1)}, u32[]{:S(2)}, u32[]{:S(2)}) collective-permute-start(bf16[128,1536]{1,0:T(8,128)(2,1)} %param.16), channel_id=1, source_target_pairs={{0,2},{1,3},{2,0},{3,1},{4,6},{5,7},{6,4},{7,5},{8,10},{9,11},{10,... | collective-permute-start | bytes 1179656 | tf_op jit(solution)/shard_map/ppermute | solution.py:628
  3.7 11.0 %collective-permute-start.3 = (bf16[8,512]{1,0:T(8,128)(2,1)}, bf16[8,512]{1,0:T(8,128)(2,1)S(1)}, u32[]{:S(2)}, u32[]{:S(2)}) collective-permute-start(bf16[8,512]{1,0:T(8,128)(2,1)} %param.20), channel_id=1, source_target_pairs={{0,1},{1,0},{2,3},{3,2},{4,5},{5,4},{6,7},{7,6},{8,9},{9,8},{10,11... | collective-permute-start | bytes 24584 | tf_op jit(solution)/shard_map/ppermute | solution.py:628
  3.9 12.5 %collective-permute-start.4 = (bf16[8,512]{1,0:T(8,128)(2,1)}, bf16[8,512]{1,0:T(8,128)(2,1)S(1)}, u32[]{:S(2)}, u32[]{:S(2)}) collective-permute-start(bf16[8,512]{1,0:T(8,128)(2,1)} %param.20), channel_id=1, source_target_pairs={{0,2},{1,3},{2,0},{3,1},{4,6},{5,7},{6,4},{7,5},{8,10},{9,11},{10,... | collective-permute-start | bytes 24584 | tf_op jit(solution)/shard_map/ppermute | solution.py:628
  4.2 13.6 %collective-permute-start.6 = (bf16[128,512]{1,0:T(8,128)(2,1)}, bf16[128,512]{1,0:T(8,128)(2,1)}, u32[]{:S(2)}, u32[]{:S(2)}) collective-permute-start(bf16[128,512]{1,0:T(8,128)(2,1)} %param.17), channel_id=1, source_target_pairs={{0,1},{1,0},{2,3},{3,2},{4,5},{5,4},{6,7},{7,6},{8,9},{9,8},{10,11... | collective-permute-start | bytes 393224 | tf_op jit(solution)/shard_map/ppermute | solution.py:628
  14.7 5.8 %collective-permute-start.7 = (bf16[128,512]{1,0:T(8,128)(2,1)S(1)}, bf16[128,512]{1,0:T(8,128)(2,1)S(1)}, u32[]{:S(2)}, u32[]{:S(2)}) collective-permute-start(bf16[128,512]{1,0:T(8,128)(2,1)S(1)} %copy-done.11), channel_id=1, source_target_pairs={{0,2},{1,3},{2,0},{3,1},{4,6},{5,7},{6,4},{7,5},{8,10},{9,11},{10,... | collective-permute-start | bytes 393224 | tf_op jit(solution)/shard_map/ppermute | solution.py:628
  16.4 1.2 collective-permute-start.5
  17.6 25.7 %collective-permute-start.9 = (bf16[128,2048]{1,0:T(8,128)(2,1)S(1)}, bf16[128,2048]{1,0:T(8,128)(2,1)S(1)}, u32[]{:S(2)}, u32[]{:S(2)}) collective-permute-start(bf16[128,2048]{1,0:T(8,128)(2,1)S(1)} %copy-done.8), channel_id=1, source_target_pairs={{0,1},{1,0},{2,3},{3,2},{4,5},{5,4},{6,7},{7,6},{8,9},{9,8},{10,11... | collective-permute-start | bytes 1572872 | tf_op jit(solution)/shard_map/ppermute | solution.py:628
  17.8 14.9 %collective-permute-start.10 = (bf16[128,2048]{1,0:T(8,128)(2,1)S(1)}, bf16[128,2048]{1,0:T(8,128)(2,1)}, u32[]{:S(2)}, u32[]{:S(2)}) collective-permute-start(bf16[128,2048]{1,0:T(8,128)(2,1)S(1)} %copy-done.8), channel_id=1, source_target_pairs={{0,2},{1,3},{2,0},{3,1},{4,6},{5,7},{6,4},{7,5},{8,10},{9,11},{10,... | collective-permute-start | bytes 1572872 | tf_op jit(solution)/shard_map/ppermute | solution.py:628
  20.5 1.3 collective-permute-start.8
  21.9 21.4 %collective-permute-start.13 = (bf16[512,512]{1,0:T(8,128)(2,1)}, bf16[512,512]{1,0:T(8,128)(2,1)}, u32[]{:S(2)}, u32[]{:S(2)}) collective-permute-start(bf16[512,512]{1,0:T(8,128)(2,1)} %param.19), channel_id=1, source_target_pairs={{0,2},{1,3},{2,0},{3,1},{4,6},{5,7},{6,4},{7,5},{8,10},{9,11},{10,... | collective-permute-start | bytes 1572872 | tf_op jit(solution)/shard_map/ppermute | solution.py:628
  24.1 20.0 %collective-permute-start.12 = (bf16[512,512]{1,0:T(8,128)(2,1)}, bf16[512,512]{1,0:T(8,128)(2,1)S(1)}, u32[]{:S(2)}, u32[]{:S(2)}) collective-permute-start(bf16[512,512]{1,0:T(8,128)(2,1)} %param.19), channel_id=1, source_target_pairs={{0,1},{1,0},{2,3},{3,2},{4,5},{5,4},{6,7},{7,6},{8,9},{9,8},{10,11... | collective-permute-start | bytes 1572872 | tf_op jit(solution)/shard_map/ppermute | solution.py:628
  24.2 24.5 %collective-permute-start.2 = (bf16[128,1536]{1,0:T(8,128)(2,1)S(1)}, bf16[128,1536]{1,0:T(8,128)(2,1)S(1)}, u32[]{:S(2)}, u32[]{:S(2)}) collective-permute-start(bf16[128,1536]{1,0:T(8,128)(2,1)S(1)} %collective-permute-done.1), channel_id=1, source_target_pairs={{0,1},{1,0},{2,3},{3,2},{4,5},{5,4},{6,7},{7,6},{8,9},{9,8},{10,11... | collective-permute-start | bytes 1179656 | tf_op jit(solution)/shard_map/ppermute | solution.py:628
  32.6 66.7 %collective-permute-start.11 = (bf16[128,2048]{1,0:T(8,128)(2,1)}, bf16[128,2048]{1,0:T(8,128)(2,1)}, u32[]{:S(2)}, u32[]{:S(2)}) collective-permute-start(bf16[128,2048]{1,0:T(8,128)(2,1)} %collective-permute-done.10), channel_id=1, source_target_pairs={{0,1},{1,0},{2,3},{3,2},{4,5},{5,4},{6,7},{7,6},{8,9},{9,8},{10,11... | collective-permute-start | bytes 1572872 | tf_op jit(solution)/shard_map/ppermute | solution.py:628
  43.3 58.0 %collective-permute-start.14 = (bf16[512,512]{1,0:T(8,128)(2,1)}, bf16[512,512]{1,0:T(8,128)(2,1)}, u32[]{:S(2)}, u32[]{:S(2)}) collective-permute-start(bf16[512,512]{1,0:T(8,128)(2,1)} %collective-permute-done.13), channel_id=1, source_target_pairs={{0,1},{1,0},{2,3},{3,2},{4,5},{5,4},{6,7},{7,6},{8,9},{9,8},{10,11... | collective-permute-start | bytes 1572872 | tf_op jit(solution)/shard_map/ppermute | solution.py:628
  241.2 24.6 %collective-permute-start.16 = (bf16[1664,512]{1,0:T(8,128)(2,1)S(1)}, bf16[1664,512]{1,0:T(8,128)(2,1)}, u32[]{:S(2)}, u32[]{:S(2)}) collective-permute-start(bf16[1664,512]{1,0:T(8,128)(2,1)S(1)} %get-tuple-element.90), channel_id=1, source_target_pairs={{0,1},{1,0},{2,3},{3,2},{4,5},{5,4},{6,7},{7,6},{8,9},{9,8},{10,11... | collective-permute-start | bytes 5111816 | tf_op jit(solution)/shard_map/ppermute | solution.py:628
  262.4 27.2 %collective-permute-start.15 = (bf16[1664,512]{1,0:T(8,128)(2,1)S(1)}, bf16[1664,512]{1,0:T(8,128)(2,1)}, u32[]{:S(2)}, u32[]{:S(2)}) collective-permute-start(bf16[1664,512]{1,0:T(8,128)(2,1)S(1)} %get-tuple-element.89), channel_id=1, source_target_pairs={{0,1},{1,0},{2,3},{3,2},{4,5},{5,4},{6,7},{7,6},{8,9},{9,8},{10,11... | collective-permute-start | bytes 5111816 | tf_op jit(solution)/shard_map/ppermute | solution.py:628
  268.2 59.1 %collective-permute-start.17 = (bf16[1664,512]{1,0:T(8,128)(2,1)S(1)}, bf16[1664,512]{1,0:T(8,128)(2,1)}, u32[]{:S(2)}, u32[]{:S(2)}) collective-permute-start(bf16[1664,512]{1,0:T(8,128)(2,1)S(1)} %fusion), channel_id=1, source_target_pairs={{0,2},{1,3},{2,0},{3,1},{4,6},{5,7},{6,4},{7,5},{8,10},{9,11},{10,... | collective-permute-start | bytes 5111816 | tf_op jit(solution)/shard_map/ppermute | solution.py:628
  330.5 20.5 %collective-permute-start.18 = (bf16[832,512]{1,0:T(8,128)(2,1)S(1)}, bf16[832,512]{1,0:T(8,128)(2,1)S(1)}, u32[]{:S(2)}, u32[]{:S(2)}) collective-permute-start(bf16[832,512]{1,0:T(8,128)(2,1)S(1)} %broadcast_select_fusion), channel_id=1, source_target_pairs={{0,4},{4,0},{8,12},{12,8},{16,20},{20,16},{24,28},{28,24},{1,5},{5... | collective-permute-start | bytes 2555912 | tf_op jit(solution)/shard_map/ppermute | solution.py:628
  351.4 10.5 %collective-permute-start.19 = (bf16[416,512]{1,0:T(8,128)(2,1)S(1)}, bf16[416,512]{1,0:T(8,128)(2,1)S(1)}, u32[]{:S(2)}, u32[]{:S(2)}) collective-permute-start(bf16[416,512]{1,0:T(8,128)(2,1)S(1)} %broadcast_select_fusion.1), channel_id=1, source_target_pairs={{0,8},{4,12},{8,0},{12,4},{16,24},{20,28},{24,16},{28,20},{1,9},{5... | collective-permute-start | bytes 1277960 | tf_op jit(solution)/shard_map/ppermute | solution.py:628
  362.1 35.0 %collective-permute-start.20 = (bf16[208,512]{1,0:T(8,128)(2,1)S(1)}, bf16[208,512]{1,0:T(8,128)(2,1)S(1)}, u32[]{:S(2)}, u32[]{:S(2)}) collective-permute-start(bf16[208,512]{1,0:T(8,128)(2,1)S(1)} %broadcast_select_fusion.2), channel_id=1, source_target_pairs={{0,16},{4,20},{8,24},{12,28},{16,0},{20,4},{24,8},{28,12},{1,17},{... | collective-permute-start | bytes 638984 | tf_op jit(solution)/shard_map/ppermute | solution.py:628
  397.2 11.7 %collective-permute-start.21 = (bf16[208,512]{1,0:T(8,128)(2,1)S(1)}, bf16[208,512]{1,0:T(8,128)(2,1)S(1)}, u32[]{:S(2)}, u32[]{:S(2)}) collective-permute-start(bf16[208,512]{1,0:T(8,128)(2,1)S(1)} %add_convert_fusion.3), channel_id=1, source_target_pairs={{0,16},{4,20},{8,24},{12,28},{16,0},{20,4},{24,8},{28,12},{1,17},{... | collective-permute-start | bytes 638984 | tf_op jit(solution)/shard_map/ppermute | solution.py:628
  409.1 10.6 %collective-permute-start.22 = (bf16[416,512]{1,0:T(8,128)(2,1)S(1)}, bf16[416,512]{1,0:T(8,128)(2,1)S(1)}, u32[]{:S(2)}, u32[]{:S(2)}) collective-permute-start(bf16[416,512]{1,0:T(8,128)(2,1)S(1)} %maximum_select_fusion.2), channel_id=1, source_target_pairs={{0,8},{4,12},{8,0},{12,4},{16,24},{20,28},{24,16},{28,20},{1,9},{5... | collective-permute-start | bytes 1277960 | tf_op jit(solution)/shard_map/ppermute | solution.py:628
  420.1 18.8 %collective-permute-start.23 = (bf16[832,512]{1,0:T(8,128)(2,1)S(1)}, bf16[832,512]{1,0:T(8,128)(2,1)S(1)}, u32[]{:S(2)}, u32[]{:S(2)}) collective-permute-start(bf16[832,512]{1,0:T(8,128)(2,1)S(1)} %maximum_select_fusion.1), channel_id=1, source_target_pairs={{0,4},{4,0},{8,12},{12,8},{16,20},{20,16},{24,28},{28,24},{1,5},{5... | collective-permute-start | bytes 2555912 | tf_op jit(solution)/shard_map/ppermute | solution.py:628
  (19 other events, 105.5 us)
